TPU v7x, 32 devices: a whole 2x2x4 slice. The times are simulated.
32 devices in a mesh: parts: 2 (over y), latent: 4 (over z), dp: 4 (over x, core).
Axes of the slice: x: 2, y: 2, z: 4, core: 2. Of those that a mesh axis runs over, the one named last changes fastest.
Arguments:
- tokens: bfloat16 [8192, 3072], P(('parts', 'latent'), 'dp'), parts along dimension 0, may hold values from -6 to 6
- target: bfloat16 [8192, 3072], P(('parts', 'latent'), 'dp'), parts along dimension 0, may hold values from -6 to 6
- enc_weight: bfloat16 [6144, 4096], P(('parts', 'dp'), 'latent'), parts along dimension 0, may hold values from -0.109375 to 0.109375
- dec_weight: bfloat16 [8192, 3072], P(('parts', 'latent'), 'dp'), parts along dimension 0, may hold values from -0.5 to 0.5
- enc_bias: float32 [8192], P(('parts', 'latent')), parts along dimension 0, may hold values from -3 to 3
- dec_bias: float32 [6144], P(('parts', 'dp')), parts along dimension 0, may hold values from -3 to 3
- active: int32 [64, 8], P(('parts', 'latent')), parts along dimension 0, may hold values from 0 to 31, as said below
- counts: int32 [64], P(('parts', 'latent')), parts along dimension 0, may hold values from 0 to 8, as said below
Outputs:
- grad_enc: bfloat16 [6144, 4096], P(('parts', 'dp'), 'latent'), parts along dimension 0
- grad_dec: bfloat16 [8192, 3072], P(('parts', 'latent'), 'dp'), parts along dimension 0
There are 2 independent parts, one for each index of `parts`. A program takes and returns all parts, laid end to end along the dimension named above; each array names one. Nothing has to cross between parts.
Inputs may be any that keep to these rules, and one draw needn't show every extreme that they name: The first counts[t] entries of row t are distinct latent block ids, the blocks active for token block t; later entries are arbitrary ids. Of the 8 token blocks of one latent index, at most one has active blocks held by any one latent index. A token block has at most 2 active blocks held by one latent index, and this is reached. All token blocks together have at most 6 pairs whose block one latent index holds, and this is reached. counts[t] is how many leading entries of row t of active are used; some token block uses all 8 entries.
All inputs are finite; a program needn't handle non-finite values.
Results may differ from a plain program's by a relative error of at most 0.018.
Values may be sent and summed in bfloat16 or wider, within the bound.
A program may use at most 128 MiB of HBM per device.

v0:
```python
import jax
import jax.numpy as jnp
from jax import lax
from jax.sharding import PartitionSpec as P

BLK = 128
MB = 2


ERROR_SCALE = 0.03125


def gelu_back(pre_sum, upstream):
    ignored, pullback = jax.vjp(lambda values: jax.nn.gelu(values, approximate=True), pre_sum)
    return pullback(upstream)[0]


def rank_pairs(flag_rows):
    before = jnp.cumsum(flag_rows, axis=1) - flag_rows
    slot_ids = jnp.arange(MB, dtype=jnp.int32)
    place_ids = jnp.arange(flag_rows.shape[1], dtype=jnp.int32)
    matches = (flag_rows[:, None, :] == 1) & (before[:, None, :] == slot_ids[None, :, None])
    places = jnp.sum(jnp.where(matches, place_ids[None, None, :], 0), axis=2)
    present = jnp.any(matches, axis=2)
    return (places, present)


def local(tokens, target, enc_weight, dec_weight, enc_bias, dec_bias, active, counts):
    owners = lax.axis_size("latent")
    features = tokens.shape[1]
    own_blocks = enc_weight.shape[1] // BLK
    block_count = counts.shape[0]
    list_pos = jnp.arange(active.shape[1], dtype=jnp.int32)
    live_entry = list_pos[None, :] < counts[:, None]
    owner_ids = jnp.arange(owners, dtype=jnp.int32)
    block_ids = jnp.arange(own_blocks, dtype=jnp.int32)
    owner_of = active // own_blocks
    place_of = active % own_blocks
    member = (
        live_entry[:, :, None, None]
        & (owner_of[:, :, None, None] == owner_ids[None, None, :, None])
        & (place_of[:, :, None, None] == block_ids[None, None, None, :])
    )
    member_any = jnp.any(member, axis=1)
    sending = jnp.any(member_any, axis=2)
    chosen = jnp.sum(
        jnp.where(sending, jnp.arange(block_count, dtype=jnp.int32)[:, None], 0), axis=0
    )
    flag_out = jnp.any(member_any, axis=0).astype(jnp.int32)
    token_rows = tokens.reshape(block_count, BLK, features)
    outgoing = jnp.take(token_rows, chosen, axis=0)
    arrived, flag_in = (
        lax.all_to_all(outgoing, "latent", split_axis=0, concat_axis=0, tiled=True),
        lax.all_to_all(flag_out, "latent", split_axis=0, concat_axis=0, tiled=True),
    )
    rows_pad = jnp.repeat(arrived, MB, axis=0)
    pair_place, pair_live = rank_pairs(flag_in)
    place_flat = pair_place.reshape(-1)
    live_flat = pair_live.reshape(-1)
    enc_blocks = jnp.take(enc_weight.reshape(features, own_blocks, BLK), place_flat, axis=1)
    dec_blocks = jnp.take(dec_weight.reshape(own_blocks, BLK, features), place_flat, axis=0)
    bias_blocks = jnp.take(enc_bias.reshape(own_blocks, BLK), place_flat, axis=0)
    live_scale = live_flat.astype(jnp.float32)[:, None, None]
    pre_part = jnp.einsum("ptd,dpl->ptl", rows_pad, enc_blocks, preferred_element_type=jnp.float32)
    pre_sum = (
        lax.psum(pre_part.astype(jnp.bfloat16), "dp").astype(jnp.float32) + bias_blocks[:, None, :]
    )
    act_list = (jax.nn.gelu(pre_sum, approximate=True) * live_scale).astype(jnp.bfloat16)
    partials = jnp.einsum(
        "srtl,srld->std",
        act_list.reshape(owners, MB, BLK, BLK),
        dec_blocks.reshape(owners, MB, BLK, features),
        preferred_element_type=jnp.float32,
    ).astype(jnp.bfloat16)
    returned = lax.all_to_all(partials, "latent", split_axis=0, concat_axis=0, tiled=True)
    selector = sending.astype(jnp.bfloat16)
    rebuilt = (
        jnp.einsum("bk,ktd->btd", selector, returned, preferred_element_type=jnp.float32)
        + dec_bias[None, None, :]
    )
    scaled_error = (
        (rebuilt - target.reshape(block_count, BLK, features).astype(jnp.float32)) * ERROR_SCALE
    ).astype(jnp.bfloat16)
    error_out = jnp.take(scaled_error, chosen, axis=0)
    errors_in = lax.all_to_all(error_out, "latent", split_axis=0, concat_axis=0, tiled=True)
    delta_pad = jnp.repeat(errors_in, MB, axis=0)
    back_part = jnp.einsum(
        "ptd,pld->ptl", delta_pad, dec_blocks, preferred_element_type=jnp.float32
    )
    back_sum = lax.psum(back_part.astype(jnp.bfloat16), "dp").astype(jnp.float32)
    pre_grad = (gelu_back(pre_sum, back_sum) * live_scale).astype(jnp.bfloat16)
    place_onehot = (
        (pair_place[:, :, None] == block_ids[None, None, :]) & pair_live[:, :, None]
    ).astype(jnp.bfloat16)
    act_placed = jnp.einsum(
        "smk,smtl->sktl",
        place_onehot,
        act_list.reshape(owners, MB, BLK, BLK),
        preferred_element_type=jnp.float32,
    ).astype(jnp.bfloat16)
    grad_dec = jnp.einsum(
        "sktl,std->kld", act_placed, errors_in, preferred_element_type=jnp.float32
    )
    grad_placed = jnp.einsum(
        "smk,smtl->sktl",
        place_onehot,
        pre_grad.reshape(owners, MB, BLK, BLK),
        preferred_element_type=jnp.float32,
    ).astype(jnp.bfloat16)
    grad_enc = jnp.einsum("std,sktl->dkl", arrived, grad_placed, preferred_element_type=jnp.float32)
    grad_enc = grad_enc.reshape(features, own_blocks * BLK).astype(jnp.bfloat16)
    grad_dec = grad_dec.reshape(own_blocks * BLK, features).astype(jnp.bfloat16)
    return (grad_enc, grad_dec)


def solution(mesh):
    placed = (
        P(("parts", "latent"), "dp"),
        P(("parts", "latent"), "dp"),
        P(("parts", "dp"), "latent"),
        P(("parts", "latent"), "dp"),
        P(("parts", "latent")),
        P(("parts", "dp")),
        P(("parts", "latent"), None),
        P(("parts", "latent")),
    )
    return jax.shard_map(
        local,
        mesh=mesh,
        in_specs=placed,
        out_specs=(P(("parts", "dp"), "latent"), P(("parts", "latent"), "dp")),
        check_vma=False,
    )
```

profile of v0, /device:TPU:0, one launch (start us, length us, event | category | flops | bytes accessed | tf_op | source)
XLA Modules:
  0.0 186.1 jit_solution(3720681679677513524)
XLA Ops:
  10.1 6.3 %all-to-all-start.1 = ((s32[4,1,8]{2,1,0:T(1,128)}), s32[4,1,8]{2,1,0:T(1,128)S(1)}, u32[]{:S(2)}, u32[]{:S(2)}) async-start(s32[4,1,8]{2,1,0:T(1,128)} %bitcast.1), calls=%async_computation.1 | async-start | bytes 4096 | tf_op jit(solution)/shard_map/all_to_all | solution.py:54
  16.5 2.0 %gather_fusion.3 = bf16[4,128,768]{2,1,0:T(8,128)(2,1)S(1)} fusion(bf16[8,128,768]{2,1,0:T(8,128)(2,1)} %bitcast.67, s32[1024]{0:T(1024)S(1)} %pad_clamp_fusion.1), kind=kCustom, calls=%fused_computation.clone | custom fusion | bytes 1572880 | tf_op jit(solution)/shard_map/jit(_take)/gather | solution.py:51
  19.5 1.7 copy.52
  21.3 1.6 copy.54
  22.8 5.2 %all-to-all-start = ((bf16[4,128,768]{2,1,0:T(8,128)(2,1)}), bf16[4,128,768]{2,1,0:T(8,128)(2,1)}, u32[]{:S(2)}, u32[]{:S(2)}) async-start(bf16[4,128,768]{2,1,0:T(8,128)(2,1)} %broadcast_select_fusion.1), calls=%async_computation | async-start | bytes 1572864 | tf_op jit(solution)/shard_map/all_to_all | solution.py:53
  29.3 1.9 %gather_fusion = bf16[8,768,128]{2,1,0:T(8,128)(2,1)} fusion(bf16[768,8,128]{2,0,1:T(8,128)(2,1)S(1)} %copy-done.1, s32[1024]{0:T(1024)S(1)} %pad_clamp_fusion), kind=kCustom, calls=%fused_computation.2 | custom fusion | bytes 3145760 | tf_op jit(solution)/shard_map/jit(_take)/gather | solution.py:60
  32.9 14.8 %all-to-all-done = bf16[4,128,768]{2,1,0:T(8,128)(2,1)} async-done(((bf16[4,128,768]{2,1,0:T(8,128)(2,1)}), bf16[4,128,768]{2,1,0:T(8,128)(2,1)}, u32[]{:S(2)}, u32[]{:S(2)}) %all-to-all-start) | async-done | bytes 786464 | tf_op jit(solution)/shard_map/all_to_all | solution.py:53
  50.8 31.2 %all-reduce.3.cloned.1.call-done = bf16[8,128,128]{2,1,0:T(8,128)(2,1)} async-done(((bf16[8,128,128]{2,1,0:T(8,128)(2,1)}), bf16[8,128,128]{2,1,0:T(8,128)(2,1)}) %all-reduce.3.cloned.1.call-update) | async-done | bytes 262160 | tf_op jit(solution)/shard_map/psum | solution.py:66
  83.8 1.4 bitcast_convert_fusion.2
  85.2 4.6 %all-to-all-start.2 = ((bf16[4,128,768]{2,1,0:T(8,128)(2,1)}), bf16[4,128,768]{2,1,0:T(8,128)(2,1)S(1)}, u32[]{:S(2)}, u32[]{:S(2)}) async-start(bf16[4,128,768]{2,1,0:T(8,128)(2,1)} %bitcast_convert_fusion.2), calls=%async_computation.2 | async-start | bytes 1572864 | tf_op jit(solution)/shard_map/all_to_all | solution.py:75
  89.8 3.4 %convert.3 = f32[8,128,768]{2,1,0:T(8,128)} convert(bf16[8,128,768]{2,1,0:T(8,128)(2,1)} %bitcast.61) | non-fusion elementwise | flops 786432 | bytes 4718592 | tf_op jit(solution)/shard_map/convert_element_type | solution.py:82
  93.2 15.6 %all-to-all-done.2 = bf16[4,128,768]{2,1,0:T(8,128)(2,1)S(1)} async-done(((bf16[4,128,768]{2,1,0:T(8,128)(2,1)}), bf16[4,128,768]{2,1,0:T(8,128)(2,1)S(1)}, u32[]{:S(2)}, u32[]{:S(2)}) %all-to-all-start.2) | async-done | bytes 786464 | tf_op jit(solution)/shard_map/all_to_all | solution.py:75
  108.8 4.2 %fusion.1 = bf16[8,128,768]{2,0,1:T(8,128)(2,1)S(1)} fusion(f32[8,128,768]{2,1,0:T(8,128)} %convert.3, f32[768]{0:T(1024)S(1)} %copy-done.7, bf16[4,128,768]{2,1,0:T(8,128)(2,1)S(1)} %all-to-all-done.2, pred[8,4]{1,0:T(8,128)(4,1)S(1)} %get-tuple-element.16), kind=kOutput, calls=%fused_computation.9 | convolution fusion | flops 9437184 | bytes 5508128 | tf_op jit(solution)/shard_map/bk,ktd->btd/dot_general | solution.py:78
  113.3 1.5 gather_fusion.4
  114.8 2.1 %broadcast_select_fusion = bf16[4,128,768]{2,1,0:T(8,128)(2,1)} fusion(bf16[4,128,768]{2,1,0:T(8,128)(2,1)} %gather_fusion.4, pred[4]{0:T(512)(128)(4,1)S(1)} %compare_and_fusion.3), kind=kLoop, calls=%fused_computation.33 | loop fusion | flops 393216 | bytes 1572868 | tf_op jit(solution)/shard_map/jit(_take)/select_n | solution.py:84
  116.9 3.5 %all-to-all-start.3 = ((bf16[4,128,768]{2,1,0:T(8,128)(2,1)}), bf16[4,128,768]{2,1,0:T(8,128)(2,1)S(1)}, u32[]{:S(2)}, u32[]{:S(2)}) async-start(bf16[4,128,768]{2,1,0:T(8,128)(2,1)} %broadcast_select_fusion), calls=%async_computation.3 | async-start | bytes 1572864 | tf_op jit(solution)/shard_map/all_to_all | solution.py:85
  120.6 1.5 convolution_convert_fusion
  122.2 17.9 %all-to-all-done.3 = bf16[4,128,768]{2,1,0:T(8,128)(2,1)S(1)} async-done(((bf16[4,128,768]{2,1,0:T(8,128)(2,1)}), bf16[4,128,768]{2,1,0:T(8,128)(2,1)S(1)}, u32[]{:S(2)}, u32[]{:S(2)}) %all-to-all-start.3) | async-done | bytes 786464 | tf_op jit(solution)/shard_map/all_to_all | solution.py:85
  141.4 1.4 fusion.14
  142.8 2.2 %bitcast_convert_fusion = bf16[8,128,768]{2,1,0:T(8,128)(2,1)} fusion(bf16[4,8,128,128]{3,1,2,0:T(8,128)(2,1)S(1)} %convolution_convert_fusion, bf16[4,128,768]{2,1,0:T(8,128)(2,1)S(1)} %all-to-all-done.3), kind=kOutput, calls=%fused_computation.5 | convolution fusion | flops 806092800 | bytes 3407872 | tf_op jit(solution)/shard_map/sktl,std->kld/dot_general | solution.py:101
  145.0 28.4 %all-reduce.5.cloned.1.call-done = bf16[8,128,128]{2,1,0:T(8,128)(2,1)} async-done(((bf16[8,128,128]{2,1,0:T(8,128)(2,1)}), bf16[8,128,128]{2,1,0:T(8,128)(2,1)}) %all-reduce.5.cloned.1.call-update) | async-done | bytes 262160 | tf_op jit(solution)/shard_map/psum | solution.py:90
  173.4 1.5 fusion.31
  175.4 2.2 %bitcast_convert_fusion.1 = bf16[768,8,128]{0,2,1:T(8,128)(2,1)S(1)} fusion(bf16[4,8,128,128]{3,1,2,0:T(8,128)(2,1)S(1)} %convolution_convert_fusion.1, bf16[4,128,768]{2,1,0:T(8,128)(2,1)} %all-to-all-done), kind=kOutput, calls=%fused_computation.6 | convolution fusion | flops 806092800 | bytes 3407872 | tf_op jit(solution)/shard_map/std,sktl->dkl/dot_general | solution.py:110
  177.6 1.6 copy.65
  (59 shorter events, 14.3 us)
Async XLA Ops:
  7.2 24.9 %copy-start = (bf16[1024,768]{1,0:T(8,128)(2,1)S(1)}, bf16[1024,768]{1,0:T(8,128)(2,1)}, u32[]{:S(2)}) copy-start(bf16[1024,768]{1,0:T(8,128)(2,1)} %param.13) | copy-start | bytes 4718596
  10.1 12.7 %all-to-all-start.1 = ((s32[4,1,8]{2,1,0:T(1,128)}), s32[4,1,8]{2,1,0:T(1,128)S(1)}, u32[]{:S(2)}, u32[]{:S(2)}) async-start(s32[4,1,8]{2,1,0:T(1,128)} %bitcast.1), calls=%async_computation.1 | async-start | bytes 4096 | tf_op jit(solution)/shard_map/all_to_all | solution.py:54
  22.8 6.4 %copy-start.1 = (bf16[768,8,128]{2,0,1:T(8,128)(2,1)S(1)}, bf16[768,8,128]{2,0,1:T(8,128)(2,1)}, u32[]{:S(2)}) copy-start(bf16[768,8,128]{2,0,1:T(8,128)(2,1)} %copy.54) | copy-start | bytes 4718596
  22.8 24.9 %all-to-all-start = ((bf16[4,128,768]{2,1,0:T(8,128)(2,1)}), bf16[4,128,768]{2,1,0:T(8,128)(2,1)}, u32[]{:S(2)}, u32[]{:S(2)}) async-start(bf16[4,128,768]{2,1,0:T(8,128)(2,1)} %broadcast_select_fusion.1), calls=%async_computation | async-start | bytes 1572864 | tf_op jit(solution)/shard_map/all_to_all | solution.py:53
  28.1 53.9 %all-reduce.3.cloned.1.call-start = ((), (), s32[]{:S(2)}) async-start(), calls=%async_computation.4 | async-start | bytes 524288 | tf_op jit(solution)/shard_map/psum | solution.py:66
  29.3 1.9 %copy-start.6 = (f32[1024]{0:T(1024)S(1)}, f32[1024]{0:T(1024)}, u32[]{:S(2)}) copy-start(f32[1024]{0:T(1024)} %param.14) | copy-start | bytes 12292
  32.7 50.4 %copy-start.2 = (bf16[8,128,768]{2,1,0:T(8,128)(2,1)}, bf16[8,128,768]{2,1,0:T(8,128)(2,1)S(1)}, u32[]{:S(2)}) copy-start(bf16[8,128,768]{2,1,0:T(8,128)(2,1)S(1)} %gather_fusion.2) | copy-start | bytes 4718596
  47.7 1.6 copy-start.4
  83.1 0.7 copy-start.5
  85.2 23.6 %all-to-all-start.2 = ((bf16[4,128,768]{2,1,0:T(8,128)(2,1)}), bf16[4,128,768]{2,1,0:T(8,128)(2,1)S(1)}, u32[]{:S(2)}, u32[]{:S(2)}) async-start(bf16[4,128,768]{2,1,0:T(8,128)(2,1)} %bitcast_convert_fusion.2), calls=%async_computation.2 | async-start | bytes 1572864 | tf_op jit(solution)/shard_map/all_to_all | solution.py:75
  89.8 19.0 %copy-start.7 = (f32[768]{0:T(1024)S(1)}, f32[768]{0:T(1024)}, u32[]{:S(2)}) copy-start(f32[768]{0:T(1024)} %param.15) | copy-start | bytes 9220
  116.9 23.1 %all-to-all-start.3 = ((bf16[4,128,768]{2,1,0:T(8,128)(2,1)}), bf16[4,128,768]{2,1,0:T(8,128)(2,1)S(1)}, u32[]{:S(2)}, u32[]{:S(2)}) async-start(bf16[4,128,768]{2,1,0:T(8,128)(2,1)} %broadcast_select_fusion), calls=%async_computation.3 | async-start | bytes 1572864 | tf_op jit(solution)/shard_map/all_to_all | solution.py:85
  120.4 52.9 %all-reduce.5.cloned.1.call-start = ((), (), s32[]{:S(2)}) async-start(), calls=%async_computation.5 | async-start | bytes 524288 | tf_op jit(solution)/shard_map/psum | solution.py:90
  140.0 1.4 copy-start.3
Sparse Core Ops, SparseCore 0:
  50.9 31.0 all-reduce.2
  142.9 30.3 all-reduce.4
where the time goes:
time: 187 us; the launch traced here: 186 us
  waiting for transfers between devices  108 us (58%)
  starting transfers between devices  19.7 us (11%)
  local copies, waits for them, and re-layouts  16.2 us (9%)
  matrix products  14.8 us (8%)
  between operations  14.2 us (8%)
  other arithmetic  13.3 us (7%)
    psum x1, waiting for transfers between devices, local(): lax.psum(pre_part.astype(jnp.bfloat16), 'dp').astype(jnp.float32)  31.2 us
    psum x1, waiting for transfers between devices, local(): lax.psum(back_part.astype(jnp.bfloat16), 'dp').astype(jnp.float32)  28.4 us
    all_to_all x1, waiting for transfers between devices, local(): lax.all_to_all(error_out, 'latent', split_axis=0, concat_axis=0, tiled=True)  17.9 us
    all_to_all x1, waiting for transfers between devices, local(): lax.all_to_all(partials, 'latent', split_axis=0, concat_axis=0, tiled=True)  15.6 us
    all_to_all x1, waiting for transfers between devices, local(): lax.all_to_all(outgoing, 'latent', split_axis=0, concat_axis=0, tiled=True)  14.8 us
    all_to_all x1, starting transfers between devices, local(): lax.all_to_all(flag_out, 'latent', split_axis=0, concat_axis=0, tiled=True)  6.32 us
    unnamed x19, local copies, waits for them, and re-layouts  5.62 us
    all_to_all x1, starting transfers between devices, local(): lax.all_to_all(outgoing, 'latent', split_axis=0, concat_axis=0, tiled=True)  5.22 us
  transfers between devices with their start and end apart: 6, of which 5 were waited for; matrix products, arithmetic and copies ran while one was open for 10% of the time, Pallas kernels for 0%

commit v1 on v0

v1 whole, which is shorter than its diff:
```python
import functools

import jax
import jax.numpy as jnp
from jax import lax
from jax.experimental import pallas as pl
from jax.experimental.pallas import tpu as pltpu
from jax.sharding import PartitionSpec as P

BLK = 128
MB = 2
ERROR_SCALE = 0.03125
GELU_C = 0.7978845608028654
GELU_A = 0.044715
CODE, TOK, PART, ERR = range(4)
RS_PRE, AG_ACT, RS_BACK, AG_GRAD = range(4)
F32 = jnp.float32
BF16 = jnp.bfloat16


def each(count, body):
    if count <= 4:
        for i in range(count):
            body(i)
    else:
        lax.fori_loop(0, count, lambda i, _: (body(i), None)[1], None)


def rows_at(block):
    return pl.ds(pl.multiple_of(block * BLK, BLK), BLK)


def unpack_source(code):
    bits = code & 255
    total = code >> 8
    two = (bits & (bits - 1)) != 0
    return bits, jnp.where(two, total >> 1, total)


def pair_masks(code, own_blocks):
    bits = code & 255
    rest = bits & (bits - 1)
    first = bits - rest
    return [
        [jnp.where(one == (1 << b), 1.0, 0.0).astype(F32) for b in range(own_blocks)]
        for one in (first, rest)
    ]


def pick(n, codes, tokens, target, outgoing, goal, sem):
    def go(k):
        _, c = unpack_source(codes[k, 0, 0])
        start = pl.ds(pl.multiple_of(c * BLK, BLK), BLK)
        pltpu.make_async_copy(tokens.at[start], outgoing.at[k], sem.at[0, k]).start()
        pltpu.make_async_copy(target.at[start], goal.at[k], sem.at[1, k]).start()

    def done(k):
        pltpu.make_async_copy(outgoing.at[k], outgoing.at[k], sem.at[0, k]).wait()
        pltpu.make_async_copy(goal.at[k], goal.at[k], sem.at[1, k]).wait()

    each(n, go)
    each(n, done)


def kernel(
    n, n_dp, groups,
    codes_hold, outgoing, goal_any, enc_any, dec_any, ebias, dbias,
    genc_any, gdec_any,
    goal, enc, dec, codes_in,
    tok, part_send, part, err_send, err,
    pre_part, pre_in, act, slope, back_part, back_in, grad, act_placed, grad_placed, genc, gdec,
    in_sem, out_sem, z_send, z_recv, d_send, d_recv,
):
    me = lax.axis_index("latent")
    q = lax.axis_index("dp")
    per = n // groups
    rows = BLK // n_dp
    features = enc.shape[0]
    own_blocks = dec.shape[0] // BLK

    loads = [
        pltpu.make_async_copy(src, dst, in_sem.at[i])
        for i, (src, dst) in enumerate(
            ((outgoing.at[me], tok.at[0]), (enc_any, enc), (dec_any, dec), (goal_any, goal))
        )
    ]
    for load in loads:
        load.start()

    barrier = pltpu.get_barrier_semaphore()

    def greet_z(j):
        pl.semaphore_signal(barrier, inc=1, device_id={"latent": lax.rem(me + j + 1, n)})

    def greet_d(j):
        pl.semaphore_signal(barrier, inc=1, device_id={"dp": lax.rem(q + j + 1, n_dp)})

    each(n - 1, greet_z)
    each(n_dp - 1, greet_d)

    def z_copy(phase, src, dst, j):
        return pltpu.make_async_remote_copy(
            src_ref=src,
            dst_ref=dst,
            send_sem=z_send.at[phase, j],
            recv_sem=z_recv.at[phase, n - j],
            device_id={"latent": lax.rem(me + j, n)},
        )

    def z_wait(phase, ref, i):
        pltpu.make_async_remote_copy(
            src_ref=ref,
            dst_ref=ref,
            send_sem=z_send.at[phase, i],
            recv_sem=z_recv.at[phase, i],
            device_id={"latent": lax.rem(me + i, n)},
        ).wait_recv()

    def d_copy(phase, g, src, dst, j):
        return pltpu.make_async_remote_copy(
            src_ref=src,
            dst_ref=dst,
            send_sem=d_send.at[phase, g, j],
            recv_sem=d_recv.at[phase, g, n_dp - j],
            device_id={"dp": lax.rem(q + j, n_dp)},
        )

    def d_wait(phase, g, ref, j):
        pltpu.make_async_remote_copy(
            src_ref=ref,
            dst_ref=ref,
            send_sem=d_send.at[phase, g, j],
            recv_sem=d_recv.at[phase, g, j],
            device_id={"dp": lax.rem(q + j, n_dp)},
        ).wait_recv()

    def span(g):
        return pl.ds(g * per, per)

    def my_rows(p):
        return pl.ds(pl.multiple_of(p * rows, rows), rows)

    def scatter(phase, g, src, dst):
        def go(k):
            j = k + 1
            peer = lax.rem(q + j, n_dp)
            d_copy(phase, g, src.at[span(g), my_rows(peer)], dst.at[n_dp - j, span(g)], j).start()

        each(n_dp - 1, go)

    def scatter_wait(phase, g, dst):
        each(n_dp - 1, lambda k: d_wait(phase, g, dst.at[k + 1, span(g)], k + 1))

    def gather(phase, g, buf):
        mine = buf.at[span(g), my_rows(q)]
        each(n_dp - 1, lambda k: d_copy(phase, g, mine, mine, k + 1).start())

    def gather_wait(phase, g, buf):
        def go(k):
            peer = lax.rem(q + k + 1, n_dp)
            d_wait(phase, g, buf.at[span(g), my_rows(peer)], k + 1)

        each(n_dp - 1, go)

    codes_in[0] = codes_hold[me]
    pl.semaphore_wait(barrier, n - 1 + n_dp - 1)

    def send_tokens(k):
        j = k + 1
        z_copy(CODE, codes_hold.at[lax.rem(me + j, n)], codes_in.at[n - j], j).start()
        z_copy(TOK, outgoing.at[lax.rem(me + j, n)], tok.at[n - j], j).start()

    each(n - 1, send_tokens)

    loads[0].wait()
    loads[1].wait()

    def arrive(g):
        def go(k):
            i = g * per + k

            def get():
                z_wait(CODE, codes_in.at[i], i)
                z_wait(TOK, tok.at[i], i)

            if isinstance(i, int):
                if i > 0:
                    get()
            else:
                pl.when(i > 0)(get)

        each(per, go)

    def at_block(i):
        return pl.ds(i * BLK, BLK) if isinstance(i, int) else rows_at(i)

    def masks_of(i):
        return pair_masks(codes_in[i, 0:1, :], own_blocks)

    def choose(i, full, dst):
        for r, mask in enumerate(masks_of(i)):
            value = mask[0] * full[:, :BLK]
            for b in range(1, own_blocks):
                value = value + mask[b] * full[:, b * BLK:(b + 1) * BLK]
            dst[i, :, r * BLK:(r + 1) * BLK] = value.astype(BF16)

    def place(i, src, dst):
        low, high = masks_of(i)
        first = src[i, :, :BLK].astype(F32)
        second = src[i, :, BLK:].astype(F32)
        for b in range(own_blocks):
            dst[at_block(i), b * BLK:(b + 1) * BLK] = (
                low[b] * first + high[b] * second
            ).astype(BF16)

    def encode(g):
        def go(k):
            i = g * per + k
            choose(i, jnp.dot(tok[i], enc[...], preferred_element_type=F32), pre_part)

        each(per, go)
        scatter(RS_PRE, g, pre_part, pre_in)

    def activate(g):
        scatter_wait(RS_PRE, g, pre_in)

        def go(k):
            i = g * per + k
            total = pre_part[i, my_rows(q), :].astype(F32)
            for j in range(1, n_dp):
                total = total + pre_in[j, i].astype(F32)
            for r, mask in enumerate(masks_of(i)):
                live = sum(mask)
                bias = sum(mask[b] * ebias[b:b + 1, :] for b in range(own_blocks))
                v = total[:, r * BLK:(r + 1) * BLK] + bias
                t = jnp.tanh(GELU_C * (v + GELU_A * (v * v * v)))
                a = 0.5 * v * (1.0 + t)
                s = 0.5 * (1.0 + t) + 0.5 * v * (1.0 - t * t) * (
                    GELU_C * (1.0 + 3.0 * GELU_A * (v * v))
                )
                act[i, my_rows(q), r * BLK:(r + 1) * BLK] = (a * live).astype(BF16)
                slope[i, :, r * BLK:(r + 1) * BLK] = s * live

        each(per, go)
        gather(AG_ACT, g, act)

    def decode(g):
        gather_wait(AG_ACT, g, act)

        def go(k):
            i = g * per + k
            place(i, act, act_placed)
            value = jnp.dot(act_placed[at_block(i), :], dec[...], preferred_element_type=F32)
            value = value.astype(BF16)

            def keep():
                part[0] = value

            def send():
                part_send[i] = value
                z_copy(PART, part_send.at[i], part.at[n - i], i).start()

            if isinstance(i, int):
                keep() if i == 0 else send()
            else:
                pl.when(i == 0)(keep)
                pl.when(i > 0)(send)

        each(per, go)

    encode(0)
    activate(0)
    loads[2].wait()
    decode(0)
    for step in range(1, groups + 2):
        if step < groups:
            arrive(step)
            encode(step)
        if 1 <= step - 1 < groups:
            activate(step - 1)
        if 1 <= step - 2 < groups:
            decode(step - 2)

    loads[3].wait()
    each(n - 1, lambda k: z_wait(PART, part.at[k + 1], k + 1))

    def rebuild(j):
        dest = lax.rem(me + j, n)
        _, c = unpack_source(codes_hold[dest, 0:1, :])

        def weight(o):
            other_bits, other = unpack_source(codes_hold[lax.rem(me + o, n), 0:1, :])
            same = jnp.where((other_bits != 0) & (other == c), 1.0, 0.0).astype(F32)
            return jnp.concatenate([same] * (features // BLK), axis=1)

        @pl.loop(0, BLK // 32)
        def _(r):
            at = pl.ds(pl.multiple_of(r * 32, 32), 32)

            def add(o, total):
                return total + weight(o) * part[o, at, :].astype(F32)

            total = jnp.zeros((32, features), F32)
            if n <= 4:
                for o in range(n):
                    total = add(o, total)
            else:
                total = lax.fori_loop(0, n, add, total)
            wanted = goal[dest, at, :].astype(F32)
            error = (((total + dbias[...]) - wanted) * ERROR_SCALE).astype(BF16)
            if isinstance(j, int) and j == 0:
                err[0, at, :] = error
            else:
                err_send[j, at, :] = error

    def rebuild_send(k):
        rebuild(k + 1)
        z_copy(ERR, err_send.at[k + 1], err.at[n - (k + 1)], k + 1).start()

    each(n - 1, rebuild_send)
    rebuild(0)

    def push_back(g):
        def go(k):
            i = g * per + k

            def get():
                z_wait(ERR, err.at[i], i)

            if isinstance(i, int):
                if i > 0:
                    get()
            else:
                pl.when(i > 0)(get)
            full = lax.dot_general(
                err[i], dec[...], (((1,), (1,)), ((), ())), preferred_element_type=F32
            )
            choose(i, full, back_part)

        each(per, go)
        scatter(RS_BACK, g, back_part, back_in)

    def make_grad(g):
        scatter_wait(RS_BACK, g, back_in)

        def go(k):
            i = g * per + k
            total = back_part[i, my_rows(q), :].astype(F32)
            for j in range(1, n_dp):
                total = total + back_in[j, i].astype(F32)
            grad[i, my_rows(q), :] = (total * slope[i]).astype(BF16)

        each(per, go)
        gather(AG_GRAD, g, grad)

    for step in range(groups):
        push_back(step)
        if step >= 1:
            make_grad(step - 1)
    make_grad(groups - 1)

    every = err[...].reshape(n * BLK, features)
    for b in range(own_blocks):
        value = lax.dot_general(
            act_placed[:, b * BLK:(b + 1) * BLK], every,
            (((0,), (0,)), ((), ())), preferred_element_type=F32,
        )
        gdec[b * BLK:(b + 1) * BLK, :] = value.astype(BF16)
    store_dec = pltpu.make_async_copy(gdec, gdec_any, out_sem.at[0])
    store_dec.start()

    for g in range(groups):
        gather_wait(AG_GRAD, g, grad)
        each(per, lambda k, g=g: place(g * per + k, grad, grad_placed))
    every = tok[...].reshape(n * BLK, features)
    for f in range(0, features, BLK):
        value = lax.dot_general(
            every[:, f:f + BLK], grad_placed[...],
            (((0,), (0,)), ((), ())), preferred_element_type=F32,
        )
        genc[f:f + BLK, :] = value.astype(BF16)
    store_enc = pltpu.make_async_copy(genc, genc_any, out_sem.at[1])
    store_enc.start()

    def settle(k):
        j = k + 1
        z_copy(CODE, codes_hold.at[lax.rem(me + j, n)], codes_in.at[n - j], j).wait_send()
        z_copy(TOK, outgoing.at[lax.rem(me + j, n)], tok.at[n - j], j).wait_send()
        z_copy(PART, part_send.at[j], part.at[n - j], j).wait_send()
        z_copy(ERR, err_send.at[j], err.at[n - j], j).wait_send()

    each(n - 1, settle)

    for g in range(groups):
        def settle_d(k, g=g):
            j = k + 1
            peer = lax.rem(q + j, n_dp)
            for phase, src, dst in ((RS_PRE, pre_part, pre_in), (RS_BACK, back_part, back_in)):
                d_copy(
                    phase, g, src.at[span(g), my_rows(peer)], dst.at[n_dp - j, span(g)], j
                ).wait_send()
            for phase, buf in ((AG_ACT, act), (AG_GRAD, grad)):
                mine = buf.at[span(g), my_rows(q)]
                d_copy(phase, g, mine, mine, j).wait_send()

        each(n_dp - 1, settle_d)
    store_dec.wait()
    store_enc.wait()


def local(tokens, target, enc_weight, dec_weight, enc_bias, dec_bias, active, counts):
    n = lax.axis_size("latent")
    n_dp = lax.axis_size("dp")
    groups = min(n, 4)
    features = tokens.shape[1]
    own = enc_weight.shape[1]
    own_blocks = own // BLK
    rows = BLK // n_dp
    position = lax.broadcasted_iota(jnp.int32, active.shape, 1)
    live = position < counts[:, None]
    value = (1 << (active % own_blocks)) + 256 * lax.broadcasted_iota(jnp.int32, active.shape, 0)
    owner_ids = jnp.arange(n, dtype=jnp.int32)
    mask = live[None] & ((active // own_blocks)[None] == owner_ids[:, None, None])
    codes = jnp.sum(jnp.where(mask, value[None], 0), axis=(1, 2))
    codes = jnp.broadcast_to(codes[:, None, None], (n, 8, BLK)).astype(jnp.int32)
    vmem = pl.BlockSpec(memory_space=pltpu.VMEM)
    hbm = pl.BlockSpec(memory_space=pl.ANY)
    slots = (n, BLK, features)
    pairs = (n, BLK, MB * BLK)
    pieces = (n_dp, n, rows, MB * BLK)
    dma = pltpu.SemaphoreType.DMA
    chosen = jax.ShapeDtypeStruct(slots, BF16)
    outgoing, goal = pl.pallas_call(
        functools.partial(pick, n),
        out_shape=(chosen, chosen),
        in_specs=[pl.BlockSpec(memory_space=pltpu.SMEM), hbm, hbm],
        out_specs=(hbm, hbm),
        scratch_shapes=[dma((2, n))],
    )(codes, tokens, target)
    return pl.pallas_call(
        functools.partial(kernel, n, n_dp, groups),
        out_shape=(
            jax.ShapeDtypeStruct(enc_weight.shape, BF16),
            jax.ShapeDtypeStruct(dec_weight.shape, BF16),
        ),
        in_specs=[vmem, hbm, hbm, hbm, hbm, vmem, vmem],
        out_specs=(hbm, hbm),
        scratch_shapes=[
            pltpu.VMEM(slots, BF16),
            pltpu.VMEM(enc_weight.shape, BF16),
            pltpu.VMEM(dec_weight.shape, BF16),
            pltpu.VMEM((n, 8, BLK), jnp.int32),
            pltpu.VMEM(slots, BF16),
            pltpu.VMEM(slots, BF16),
            pltpu.VMEM(slots, BF16),
            pltpu.VMEM(slots, BF16),
            pltpu.VMEM(slots, BF16),
            pltpu.VMEM(pairs, BF16),
            pltpu.VMEM(pieces, BF16),
            pltpu.VMEM(pairs, BF16),
            pltpu.VMEM((n, rows, MB * BLK), F32),
            pltpu.VMEM(pairs, BF16),
            pltpu.VMEM(pieces, BF16),
            pltpu.VMEM(pairs, BF16),
            pltpu.VMEM((n * BLK, own), BF16),
            pltpu.VMEM((n * BLK, own), BF16),
            pltpu.VMEM(enc_weight.shape, BF16),
            pltpu.VMEM(dec_weight.shape, BF16),
            dma((4,)),
            dma((2,)),
            dma((4, n)),
            dma((4, n)),
            dma((4, groups, n_dp)),
            dma((4, groups, n_dp)),
        ],
        compiler_params=pltpu.CompilerParams(
            collective_id=0, has_side_effects=True, vmem_limit_bytes=56 * 1024 * 1024
        ),
    )(
        codes, outgoing, goal, enc_weight, dec_weight,
        enc_bias.reshape(own_blocks, BLK), dec_bias.reshape(1, features),
    )


def solution(mesh):
    placed = (
        P(("parts", "latent"), "dp"),
        P(("parts", "latent"), "dp"),
        P(("parts", "dp"), "latent"),
        P(("parts", "latent"), "dp"),
        P(("parts", "latent")),
        P(("parts", "dp")),
        P(("parts", "latent"), None),
        P(("parts", "latent")),
    )
    return jax.shard_map(
        local,
        mesh=mesh,
        in_specs=placed,
        out_specs=(P(("parts", "dp"), "latent"), P(("parts", "latent"), "dp")),
        check_vma=False,
    )
```

time: 187 us -> 134 us (0.72)
  the two profiles are of different devices: /device:TPU:0 before, /device:TPU:17 now
where the time goes in v1:
time: 134 us
  Pallas kernels  125 us (93%)
  local copies, waits for them, and re-layouts  5.9 us (4%)
  other arithmetic  1.65 us (1%)
    pallas_call x1, Pallas kernels, local(): pl.pallas_call(functools.partial(kernel, n, n_dp, groups), out_shape=(jax...  75.5 us
    pallas_call x1, Pallas kernels, local(): pl.pallas_call(functools.partial(pick, n), out_shape=(chosen, chosen), in...  49.7 us
    unnamed x4, local copies, waits for them, and re-layouts  3.93 us

profile of v1, /device:TPU:17, one launch (start us, length us, event | category | flops | bytes accessed | tf_op | source)
XLA Modules:
  0.0 133.5 jit_solution(7973473368395274073)
XLA Ops:
  0.6 0.7 iota_compare_fusion.1
  1.4 1.3 reshape.29.dbias
  2.6 0.8 add_select_fusion.1
  3.4 0.2 select_reduce_fusion
  3.6 0.7 broadcast_in_dim.16.codes.codes_hold
  4.3 49.7 %shard_map.95 = (bf16[4,128,768]{2,1,0:T(8,128)(2,1)}, bf16[4,128,768]{2,1,0:T(8,128)(2,1)}) custom-call(s32[4,8,128]{2,1,0:T(8,128)} %broadcast_in_dim.16.codes.codes_hold, bf16[1024,768]{1,0:T(8,128)(2,1)} %tokens.1, bf16[1024,768]{1,0:T(8,128)(2,1)} %target.1), custom_call_target="tpu_custom_call" | custom-call | tf_op jit(solution)/shard_map/pallas_call | solution.py:433
  54.0 75.5 %shard_map.96 = (bf16[768,1024]{1,0:T(8,128)(2,1)}, bf16[1024,768]{1,0:T(8,128)(2,1)}) custom-call(s32[4,8,128]{2,1,0:T(8,128)} %broadcast_in_dim.16.codes.codes_hold, bf16[4,128,768]{2,1,0:T(8,128)(2,1)} %get-tuple-element.4.outgoing, bf16[4,128,768]{2,1,0:T(8,128)(2,1)} %get-tuple-element.5.goal_any, bf16[768,1024]{1,0:T(8,128)(2,1)} %enc_any.1, ...), custom_call_target="tpu_custom_call" | custom-call | tf_op jit(solution)/shard_map/pallas_call | solution.py:440
  129.6 0.0 copy-start
  129.6 2.8 %copy.12 = bf16[768,1024]{1,0:T(8,128)(2,1)} copy(bf16[768,1024]{1,0:T(8,128)(2,1)} %get-tuple-element.10) | data formatting | bytes 3145728
  132.4 0.0 copy-done
  132.4 1.1 copy.13
  (1 shorter events, 0.0 us)
Async XLA Ops:
  129.6 2.8 %copy-start = (bf16[1024,768]{1,0:T(8,128)(2,1)S(1)}, bf16[1024,768]{1,0:T(8,128)(2,1)}, u32[]{:S(2)}) copy-start(bf16[1024,768]{1,0:T(8,128)(2,1)} %get-tuple-element.11) | copy-start | bytes 4718596

commit v2 on v0

v2 whole, which is shorter than its diff:
```python
import functools

import jax
import jax.numpy as jnp
from jax import lax
from jax.experimental import pallas as pl
from jax.experimental.pallas import tpu as pltpu
from jax.sharding import PartitionSpec as P

BLK = 128
MB = 2
ERROR_SCALE = 0.03125
GELU_C = 0.7978845608028654
GELU_A = 0.044715
TOK, PART, ERR = range(3)
RS_PRE, AG_ACT, RS_BACK, AG_GRAD = range(4)
F32 = jnp.float32
BF16 = jnp.bfloat16


def each(count, body):
    if count <= 4:
        for i in range(count):
            body(i)
    else:
        lax.fori_loop(0, count, lambda i, _: (body(i), None)[1], None)


def pair_masks(code, own_blocks):
    bits = code & 255
    rest = bits & (bits - 1)
    first = bits - rest
    return [
        [jnp.where(one == (1 << b), 1.0, 0.0).astype(F32) for b in range(own_blocks)]
        for one in (first, rest)
    ]


def kernel(
    n, n_dp, halves,
    counts, active, tokens_any, target_any, enc_any, dec_any, ebias, dbias,
    genc_any, gdec_any,
    tokens, target, enc, dec, codes_out, codes_in,
    tok_send, goal, tok, part_send, part, err_send, err,
    pre_part, pre_in, act, slope, back_part, back_in, grad, act_placed, grad_placed, genc, gdec,
    in_sem, out_sem, c_send, c_recv, z_send, z_recv, d_send, d_recv,
):
    me = lax.axis_index("latent")
    q = lax.axis_index("dp")
    high = BLK // halves
    rows = high // n_dp
    features = enc.shape[0]
    own_blocks = dec.shape[0] // BLK
    blocks, width = active.shape
    tile = min(n, 4)

    loads = [
        pltpu.make_async_copy(src, dst, in_sem.at[i])
        for i, (src, dst) in enumerate(
            ((tokens_any, tokens), (enc_any, enc), (dec_any, dec), (target_any, target))
        )
    ]
    for load in loads:
        load.start()

    barrier = pltpu.get_barrier_semaphore()

    def greet_z(j):
        pl.semaphore_signal(barrier, inc=1, device_id={"latent": lax.rem(me + j + 1, n)})

    def greet_d(j):
        pl.semaphore_signal(barrier, inc=1, device_id={"dp": lax.rem(q + j + 1, n_dp)})

    each(n - 1, greet_z)
    each(n_dp - 1, greet_d)

    row = lax.broadcasted_iota(jnp.int32, (blocks, width), 0)
    column = lax.broadcasted_iota(jnp.int32, (blocks, width), 1)
    used = jnp.zeros((blocks, width), jnp.int32)
    for t in range(blocks):
        used = jnp.where(row == t, counts[t], used)
    ids = active[...]
    place_bit = jnp.zeros((blocks, width), jnp.int32)
    for b in range(own_blocks):
        place_bit = jnp.where(ids % own_blocks == b, 1 << b, place_bit)
    value = (place_bit + 256 * row).astype(F32)
    owner = ids // own_blocks

    def encode_owner(k):
        total = jnp.where((column < used) & (owner == k), value, 0.0)
        total = jnp.sum(jnp.sum(total, axis=1, keepdims=True), axis=0, keepdims=True)
        codes_out[k] = jnp.broadcast_to(total, (8, BLK)).astype(jnp.int32)

    each(n, encode_owner)
    codes_in[0] = codes_out[me]

    def source(j):
        code = codes_out[lax.rem(me + j, n), 0:1, :]
        bits = code & 255
        total = code >> 8
        two = (bits & (bits - 1)) != 0
        return bits, jnp.where(two, total >> 1, total)

    def wide(mask):
        return jnp.concatenate([mask] * (features // BLK), axis=1)

    def chosen_rows(j, ref, at):
        _, c = source(j)
        total = None
        for t in range(blocks):
            weight = wide(jnp.where(c == t, 1.0, 0.0).astype(BF16))
            piece = weight * ref[t * BLK + at:t * BLK + at + 32, :]
            total = piece if total is None else total + piece
        return total

    def z_copy(phase, h, src, dst, j):
        return pltpu.make_async_remote_copy(
            src_ref=src.at[h, j],
            dst_ref=dst.at[h, n - j],
            send_sem=z_send.at[phase, h, j],
            recv_sem=z_recv.at[phase, h, n - j],
            device_id={"latent": lax.rem(me + j, n)},
        )

    def c_copy(j):
        return pltpu.make_async_remote_copy(
            src_ref=codes_out.at[lax.rem(me + j, n)],
            dst_ref=codes_in.at[n - j],
            send_sem=c_send.at[j],
            recv_sem=c_recv.at[n - j],
            device_id={"latent": lax.rem(me + j, n)},
        )

    def z_wait(phase, h, ref):
        each(n - 1, lambda k: pltpu.make_async_remote_copy(
            src_ref=ref.at[h, k + 1],
            dst_ref=ref.at[h, k + 1],
            send_sem=z_send.at[phase, h, k + 1],
            recv_sem=z_recv.at[phase, h, k + 1],
            device_id={"latent": lax.rem(me + k + 1, n)},
        ).wait_recv())

    def c_wait(j):
        pltpu.make_async_remote_copy(
            src_ref=codes_in.at[j],
            dst_ref=codes_in.at[j],
            send_sem=c_send.at[j],
            recv_sem=c_recv.at[j],
            device_id={"latent": lax.rem(me + j, n)},
        ).wait_recv()

    def d_copy(phase, h, src, dst, j):
        return pltpu.make_async_remote_copy(
            src_ref=src,
            dst_ref=dst,
            send_sem=d_send.at[phase, h, j],
            recv_sem=d_recv.at[phase, h, n_dp - j],
            device_id={"dp": lax.rem(q + j, n_dp)},
        )

    def d_wait(phase, h, ref, j):
        pltpu.make_async_remote_copy(
            src_ref=ref,
            dst_ref=ref,
            send_sem=d_send.at[phase, h, j],
            recv_sem=d_recv.at[phase, h, j],
            device_id={"dp": lax.rem(q + j, n_dp)},
        ).wait_recv()

    every = pl.ds(0, n)

    def dp_rows(p):
        return pl.ds(pl.multiple_of(p * rows, rows), rows)

    def scatter_copy(phase, h, src, dst, j):
        peer = lax.rem(q + j, n_dp)
        return d_copy(phase, h, src.at[h, every, dp_rows(peer)], dst.at[h, n_dp - j], j)

    def scatter(phase, h, src, dst):
        each(n_dp - 1, lambda k: scatter_copy(phase, h, src, dst, k + 1).start())

    def scatter_wait(phase, h, dst):
        each(n_dp - 1, lambda k: d_wait(phase, h, dst.at[h, k + 1], k + 1))

    def gather_copy(phase, h, buf, j):
        mine = buf.at[h, every, dp_rows(q)]
        return d_copy(phase, h, mine, mine, j)

    def gather(phase, h, buf):
        each(n_dp - 1, lambda k: gather_copy(phase, h, buf, k + 1).start())

    def gather_wait(phase, h, buf):
        each(n_dp - 1, lambda k: d_wait(
            phase, h, buf.at[h, every, dp_rows(lax.rem(q + k + 1, n_dp))], k + 1
        ))

    loads[0].wait()
    for h in range(halves):
        def stage(j, h=h):
            for at in range(0, high, 32):
                tok_send[h, j, at:at + 32, :] = chosen_rows(j, tokens, h * high + at)

        each(n - 1, lambda k: stage(k + 1))
        if h == 0:
            pl.semaphore_wait(barrier, n - 1 + n_dp - 1)
            each(n - 1, lambda k: c_copy(k + 1).start())
        each(n - 1, lambda k, h=h: z_copy(TOK, h, tok_send, tok, k + 1).start())
    for h in range(halves):
        for at in range(0, high, 32):
            tok[h, 0, at:at + 32, :] = chosen_rows(0, tokens, h * high + at)
    loads[3].wait()

    def aim(j):
        for h in range(halves):
            for at in range(0, high, 32):
                goal[h, j, at:at + 32, :] = chosen_rows(j, target, h * high + at)

    each(n, aim)
    loads[1].wait()
    each(n - 1, lambda k: c_wait(k + 1))
    loads[2].wait()

    def masks_of(i):
        return pair_masks(codes_in[i, 0:1, :], own_blocks)

    def tiles(body):
        each(n // tile, lambda k: body(k * tile))

    def stack(h, buf, first):
        block = buf[h, pl.ds(first, tile)]
        return block.reshape(tile * high, block.shape[-1])

    def choose(h, i, full, dst):
        for r, mask in enumerate(masks_of(i)):
            total = mask[0] * full[:, :BLK]
            for b in range(1, own_blocks):
                total = total + mask[b] * full[:, b * BLK:(b + 1) * BLK]
            dst[h, i, :, r * BLK:(r + 1) * BLK] = total.astype(BF16)

    def place(h, i, src, dst):
        low, rest = masks_of(i)
        first = src[h, i, :, :BLK].astype(F32)
        second = src[h, i, :, BLK:].astype(F32)
        for b in range(own_blocks):
            dst[h, i, :, b * BLK:(b + 1) * BLK] = (
                low[b] * first + rest[b] * second
            ).astype(BF16)

    def encode(h):
        z_wait(TOK, h, tok)

        def go(first):
            full = jnp.dot(stack(h, tok, first), enc[...], preferred_element_type=F32)
            for k in range(tile):
                choose(h, first + k, full[k * high:(k + 1) * high], pre_part)

        tiles(go)
        scatter(RS_PRE, h, pre_part, pre_in)

    def activate(h):
        scatter_wait(RS_PRE, h, pre_in)

        def go(i):
            total = pre_part[h, i, dp_rows(q), :].astype(F32)
            for j in range(1, n_dp):
                total = total + pre_in[h, j, i].astype(F32)
            for r, mask in enumerate(masks_of(i)):
                live = sum(mask)
                bias = sum(mask[b] * ebias[b:b + 1, :] for b in range(own_blocks))
                v = total[:, r * BLK:(r + 1) * BLK] + bias
                t = jnp.tanh(GELU_C * (v + GELU_A * (v * v * v)))
                a = 0.5 * v * (1.0 + t)
                s = 0.5 * (1.0 + t) + 0.5 * v * (1.0 - t * t) * (
                    GELU_C * (1.0 + 3.0 * GELU_A * (v * v))
                )
                act[h, i, dp_rows(q), r * BLK:(r + 1) * BLK] = (a * live).astype(BF16)
                slope[h, i, :, r * BLK:(r + 1) * BLK] = s * live

        each(n, go)
        gather(AG_ACT, h, act)

    def decode(h):
        gather_wait(AG_ACT, h, act)

        def go(first):
            for k in range(tile):
                place(h, first + k, act, act_placed)
            full = jnp.dot(stack(h, act_placed, first), dec[...], preferred_element_type=F32)
            full = full.astype(BF16)
            for k in range(tile):
                part_send[h, first + k] = full[k * high:(k + 1) * high]

        tiles(go)
        part[h, 0] = part_send[h, 0]
        each(n - 1, lambda k: z_copy(PART, h, part_send, part, k + 1).start())

    for h in range(halves):
        encode(h)
        activate(h)
        decode(h)

    def rebuild(h):
        z_wait(PART, h, part)

        def go(j):
            _, c = source(j)

            def weight(o):
                other_bits, other = source(o)
                return wide(jnp.where((other_bits != 0) & (other == c), 1.0, 0.0).astype(F32))

            for at in range(0, high, 16):
                def add(o, total, at=at):
                    return total + weight(o) * part[h, o, at:at + 16, :].astype(F32)

                total = jnp.zeros((16, features), F32)
                if n <= 4:
                    for o in range(n):
                        total = add(o, total)
                else:
                    total = lax.fori_loop(0, n, add, total)
                wanted = goal[h, j, at:at + 16, :].astype(F32)
                err_send[h, j, at:at + 16, :] = (
                    ((total + dbias[...]) - wanted) * ERROR_SCALE
                ).astype(BF16)

        def send(k):
            go(k + 1)
            z_copy(ERR, h, err_send, err, k + 1).start()

        each(n - 1, send)
        go(0)
        err[h, 0] = err_send[h, 0]

    for h in range(halves):
        rebuild(h)

    def push_back(h):
        z_wait(ERR, h, err)

        def go(first):
            full = lax.dot_general(
                stack(h, err, first), dec[...], (((1,), (1,)), ((), ())),
                preferred_element_type=F32,
            )
            for k in range(tile):
                choose(h, first + k, full[k * high:(k + 1) * high], back_part)

        tiles(go)
        scatter(RS_BACK, h, back_part, back_in)

    def make_grad(h):
        scatter_wait(RS_BACK, h, back_in)

        def go(i):
            total = back_part[h, i, dp_rows(q), :].astype(F32)
            for j in range(1, n_dp):
                total = total + back_in[h, j, i].astype(F32)
            grad[h, i, dp_rows(q), :] = (total * slope[h, i]).astype(BF16)

        each(n, go)
        gather(AG_GRAD, h, grad)

    for h in range(halves):
        push_back(h)
        make_grad(h)

    depth = halves * n * high
    errors = err[...].reshape(depth, features)
    for b in range(own_blocks):
        left = act_placed[:, :, :, b * BLK:(b + 1) * BLK].reshape(depth, BLK)
        gdec[b * BLK:(b + 1) * BLK, :] = lax.dot_general(
            left, errors, (((0,), (0,)), ((), ())), preferred_element_type=F32
        ).astype(BF16)
    store_dec = pltpu.make_async_copy(gdec, gdec_any, out_sem.at[0])
    store_dec.start()

    for h in range(halves):
        gather_wait(AG_GRAD, h, grad)
        each(n, lambda i, h=h: place(h, i, grad, grad_placed))
    right = grad_placed[...].reshape(depth, own_blocks * BLK)
    for f in range(0, features, BLK):
        left = tok[:, :, :, f:f + BLK].reshape(depth, BLK)
        genc[f:f + BLK, :] = lax.dot_general(
            left, right, (((0,), (0,)), ((), ())), preferred_element_type=F32
        ).astype(BF16)
    store_enc = pltpu.make_async_copy(genc, genc_any, out_sem.at[1])
    store_enc.start()

    each(n - 1, lambda k: c_copy(k + 1).wait_send())
    for h in range(halves):
        def settle_z(k, h=h):
            for phase, src, dst in (
                (TOK, tok_send, tok), (PART, part_send, part), (ERR, err_send, err)
            ):
                z_copy(phase, h, src, dst, k + 1).wait_send()

        def settle_d(k, h=h):
            for phase, src, dst in ((RS_PRE, pre_part, pre_in), (RS_BACK, back_part, back_in)):
                scatter_copy(phase, h, src, dst, k + 1).wait_send()
            for phase, buf in ((AG_ACT, act), (AG_GRAD, grad)):
                gather_copy(phase, h, buf, k + 1).wait_send()

        each(n - 1, settle_z)
        each(n_dp - 1, settle_d)
    store_dec.wait()
    store_enc.wait()


def local(tokens, target, enc_weight, dec_weight, enc_bias, dec_bias, active, counts):
    n = lax.axis_size("latent")
    n_dp = lax.axis_size("dp")
    halves = max(1, BLK // (16 * n_dp))
    features = tokens.shape[1]
    own = enc_weight.shape[1]
    high = BLK // halves
    rows = high // n_dp
    vmem = pl.BlockSpec(memory_space=pltpu.VMEM)
    smem = pl.BlockSpec(memory_space=pltpu.SMEM)
    hbm = pl.BlockSpec(memory_space=pl.ANY)
    slots = pltpu.VMEM((halves, n, high, features), BF16)
    pairs = pltpu.VMEM((halves, n, high, MB * BLK), BF16)
    pieces = pltpu.VMEM((halves, n_dp, n, rows, MB * BLK), BF16)
    placed = pltpu.VMEM((halves, n, high, own), BF16)
    codes = pltpu.VMEM((n, 8, BLK), jnp.int32)
    dma = pltpu.SemaphoreType.DMA
    return pl.pallas_call(
        functools.partial(kernel, n, n_dp, halves),
        out_shape=(
            jax.ShapeDtypeStruct(enc_weight.shape, BF16),
            jax.ShapeDtypeStruct(dec_weight.shape, BF16),
        ),
        in_specs=[smem, vmem, hbm, hbm, hbm, hbm, vmem, vmem],
        out_specs=(hbm, hbm),
        scratch_shapes=[
            pltpu.VMEM(tokens.shape, BF16),
            pltpu.VMEM(target.shape, BF16),
            pltpu.VMEM(enc_weight.shape, BF16),
            pltpu.VMEM(dec_weight.shape, BF16),
            codes,
            codes,
            slots,
            slots,
            slots,
            slots,
            slots,
            slots,
            slots,
            pairs,
            pieces,
            pairs,
            pltpu.VMEM((halves, n, rows, MB * BLK), F32),
            pairs,
            pieces,
            pairs,
            placed,
            placed,
            pltpu.VMEM(enc_weight.shape, BF16),
            pltpu.VMEM(dec_weight.shape, BF16),
            dma((4,)),
            dma((2,)),
            dma((n,)),
            dma((n,)),
            dma((3, halves, n)),
            dma((3, halves, n)),
            dma((4, halves, n_dp)),
            dma((4, halves, n_dp)),
        ],
        compiler_params=pltpu.CompilerParams(
            collective_id=0, has_side_effects=True, vmem_limit_bytes=60 * 1024 * 1024
        ),
    )(
        counts, active, tokens, target, enc_weight, dec_weight,
        enc_bias.reshape(own // BLK, BLK), dec_bias.reshape(1, features),
    )


def solution(mesh):
    placed = (
        P(("parts", "latent"), "dp"),
        P(("parts", "latent"), "dp"),
        P(("parts", "dp"), "latent"),
        P(("parts", "latent"), "dp"),
        P(("parts", "latent")),
        P(("parts", "dp")),
        P(("parts", "latent"), None),
        P(("parts", "latent")),
    )
    return jax.shard_map(
        local,
        mesh=mesh,
        in_specs=placed,
        out_specs=(P(("parts", "dp"), "latent"), P(("parts", "latent"), "dp")),
        check_vma=False,
    )
```

time: 187 us -> 76.5 us (0.41)
  waiting for transfers between devices: 108 us -> 0 us
  Pallas kernels: 0 us -> 69.5 us
  starting transfers between devices: 19.7 us -> 0 us
  matrix products: 14.8 us -> 0 us
  between operations: 14.2 us -> 0.65 us
  other arithmetic: 13.3 us -> 0 us
  local copies, waits for them, and re-layouts: 16.2 us -> 5.2 us
    pallas_call x0 -> x1, Pallas kernels: none -> 69.5 us  [local(): pl.pallas_call(functools.partial(kernel, n, n_dp, halves), out_shape=(jax...]
    psum x2 -> x0, waiting for transfers between devices: 59.5 us -> none  [the longest x1 31.2 us: local(): lax.psum(pre_part.astype(jnp.bfloat16), 'dp').astype(jnp.float32)]
    all_to_all x4 -> x0, waiting for transfers between devices: 48.3 us -> none  [the longest x1 17.9 us: local(): lax.all_to_all(error_out, 'latent', split_axis=0, concat_axis=0, tiled=True)]
    all_to_all x4 -> x0, starting transfers between devices: 19.6 us -> none  [the longest x1 6.32 us: local(): lax.all_to_all(flag_out, 'latent', split_axis=0, concat_axis=0, tiled=True)]
    dot_general x8 -> x0, matrix products: 14.8 us -> none  [the longest x1 4.24 us: local(): jnp.einsum('bk,ktd->btd', selector, returned, preferred_element_type=jnp....]
    convert_element_type x5 -> x0, other arithmetic: 6.6 us -> none  [the longest x1 3.36 us: local(): target.reshape(block_count, BLK, features).astype(jnp.float32)]
    gather x5 -> x0, local copies, waits for them, and re-layouts: 6.59 us -> none  [the longest x1 2.01 us: local(): outgoing = jnp.take(token_rows, chosen, axis=0)]
    select_n x6 -> x0, other arithmetic: 4.07 us -> none  [the longest x1 2.15 us: local(): error_out = jnp.take(scaled_error, chosen, axis=0)]
  transfers between devices with their start and end apart: 6 -> 0, of which waited for: 5 -> 0; matrix products, arithmetic and copies ran while one was open for 10% -> 0% of each run, Pallas kernels for 0% -> 0%
where the time goes in v2:
time: 76.5 us; the launch traced here: 75.3 us
  Pallas kernels  69.5 us (91%)
  local copies, waits for them, and re-layouts  5.2 us (7%)
    pallas_call x1, Pallas kernels, local(): pl.pallas_call(functools.partial(kernel, n, n_dp, halves), out_shape=(jax...  69.5 us
    unnamed x4, local copies, waits for them, and re-layouts  3.93 us

profile of v2, /device:TPU:0, one launch (start us, length us, event | category | flops | bytes accessed | tf_op | source)
XLA Modules:
  0.0 75.3 jit_solution(5692467349919376470)
XLA Ops:
  0.6 1.3 %reshape.11.dbias = f32[1,768]{1,0:T(1,128)} reshape(f32[768]{0:T(1024)} %param.13) | data formatting | bytes 6144 | tf_op jit(solution)/shard_map/reshape | solution.py:474
  1.9 69.5 %shard_map.95 = (bf16[768,1024]{1,0:T(8,128)(2,1)}, bf16[1024,768]{1,0:T(8,128)(2,1)}) custom-call(s32[8]{0:T(128)} %counts.1, s32[8,8]{1,0:T(8,128)} %active.1, bf16[1024,768]{1,0:T(8,128)(2,1)} %tokens_any.1, bf16[1024,768]{1,0:T(8,128)(2,1)} %target_any.1, bf16[768,1024]{1,0:T(8,128)(2,1)} %enc_any.1, bf16[1024,768]{1,0:T(8,128)(2,1)} %dec_any.1, ...), custom_call_target="tpu_custom_call" | custom-call | tf_op jit(solution)/shard_map/pallas_call | solution.py:427
  71.4 0.0 copy-start
  71.4 2.8 %copy.12 = bf16[768,1024]{1,0:T(8,128)(2,1)} copy(bf16[768,1024]{1,0:T(8,128)(2,1)} %get-tuple-element.4) | data formatting | bytes 3145728
  74.2 0.0 copy-done
  74.2 1.1 %copy.13 = bf16[1024,768]{1,0:T(8,128)(2,1)} copy(bf16[1024,768]{1,0:T(8,128)(2,1)S(1)} %copy-done) | data formatting | bytes 3145728
Async XLA Ops:
  71.4 2.8 %copy-start = (bf16[1024,768]{1,0:T(8,128)(2,1)S(1)}, bf16[1024,768]{1,0:T(8,128)(2,1)}, u32[]{:S(2)}) copy-start(bf16[1024,768]{1,0:T(8,128)(2,1)} %get-tuple-element.5) | copy-start | bytes 4718596

commit v3 on v2

--- a/solution.py
+++ b/solution.py
@@ -39,10 +39,10 @@
 def kernel(
     n, n_dp, halves,
     counts, active, tokens_any, target_any, enc_any, dec_any, ebias, dbias,
-    genc_any, gdec_any,
+    tok_any, err_any, act_any, grad_any,
     tokens, target, enc, dec, codes_out, codes_in,
     tok_send, goal, tok, part_send, part, err_send, err,
-    pre_part, pre_in, act, slope, back_part, back_in, grad, act_placed, grad_placed, genc, gdec,
+    pre_part, pre_in, act, slope, back_part, back_in, grad, act_placed, grad_placed,
     in_sem, out_sem, c_send, c_recv, z_send, z_recv, d_send, d_recv,
 ):
     me = lax.axis_index("latent")
@@ -219,6 +219,9 @@
     loads[1].wait()
     each(n - 1, lambda k: c_wait(k + 1))
     loads[2].wait()
+
+    def store(which, h, src, dst):
+        return pltpu.make_async_copy(src.at[h], dst.at[h], out_sem.at[which, h])
 
     def masks_of(i):
         return pair_masks(codes_in[i, 0:1, :], own_blocks)
@@ -298,6 +301,12 @@
         encode(h)
         activate(h)
         decode(h)
+        store(0, h, tok, tok_any).start()
+        store(1, h, act_placed, act_any).start()
+
+    bias = jnp.concatenate(
+        [dbias[b:b + 1, :] for b in range(features // BLK)], axis=1
+    )
 
     def rebuild(h):
         z_wait(PART, h, part)
@@ -321,7 +330,7 @@
                     total = lax.fori_loop(0, n, add, total)
                 wanted = goal[h, j, at:at + 16, :].astype(F32)
                 err_send[h, j, at:at + 16, :] = (
-                    ((total + dbias[...]) - wanted) * ERROR_SCALE
+                    ((total + bias) - wanted) * ERROR_SCALE
                 ).astype(BF16)
 
         def send(k):
@@ -363,29 +372,13 @@
 
     for h in range(halves):
         push_back(h)
+        store(2, h, err, err_any).start()
         make_grad(h)
-
-    depth = halves * n * high
-    errors = err[...].reshape(depth, features)
-    for b in range(own_blocks):
-        left = act_placed[:, :, :, b * BLK:(b + 1) * BLK].reshape(depth, BLK)
-        gdec[b * BLK:(b + 1) * BLK, :] = lax.dot_general(
-            left, errors, (((0,), (0,)), ((), ())), preferred_element_type=F32
-        ).astype(BF16)
-    store_dec = pltpu.make_async_copy(gdec, gdec_any, out_sem.at[0])
-    store_dec.start()
 
     for h in range(halves):
         gather_wait(AG_GRAD, h, grad)
         each(n, lambda i, h=h: place(h, i, grad, grad_placed))
-    right = grad_placed[...].reshape(depth, own_blocks * BLK)
-    for f in range(0, features, BLK):
-        left = tok[:, :, :, f:f + BLK].reshape(depth, BLK)
-        genc[f:f + BLK, :] = lax.dot_general(
-            left, right, (((0,), (0,)), ((), ())), preferred_element_type=F32
-        ).astype(BF16)
-    store_enc = pltpu.make_async_copy(genc, genc_any, out_sem.at[1])
-    store_enc.start()
+        store(3, h, grad_placed, grad_any).start()
 
     each(n - 1, lambda k: c_copy(k + 1).wait_send())
     for h in range(halves):
@@ -403,8 +396,11 @@
 
         each(n - 1, settle_z)
         each(n_dp - 1, settle_d)
-    store_dec.wait()
-    store_enc.wait()
+    for h in range(halves):
+        for which, (src, dst) in enumerate((
+            (tok, tok_any), (act_placed, act_any), (err, err_any), (grad_placed, grad_any)
+        )):
+            store(which, h, src, dst).wait()
 
 
 def local(tokens, target, enc_weight, dec_weight, enc_bias, dec_bias, active, counts):
@@ -424,14 +420,13 @@
     placed = pltpu.VMEM((halves, n, high, own), BF16)
     codes = pltpu.VMEM((n, 8, BLK), jnp.int32)
     dma = pltpu.SemaphoreType.DMA
-    return pl.pallas_call(
+    arrived = jax.ShapeDtypeStruct((halves, n, high, features), BF16)
+    spread = jax.ShapeDtypeStruct((halves, n, high, own), BF16)
+    rows_in, errors_in, acts, grads = pl.pallas_call(
         functools.partial(kernel, n, n_dp, halves),
-        out_shape=(
-            jax.ShapeDtypeStruct(enc_weight.shape, BF16),
-            jax.ShapeDtypeStruct(dec_weight.shape, BF16),
-        ),
+        out_shape=(arrived, arrived, spread, spread),
         in_specs=[smem, vmem, hbm, hbm, hbm, hbm, vmem, vmem],
-        out_specs=(hbm, hbm),
+        out_specs=(hbm, hbm, hbm, hbm),
         scratch_shapes=[
             pltpu.VMEM(tokens.shape, BF16),
             pltpu.VMEM(target.shape, BF16),
@@ -455,10 +450,8 @@
             pairs,
             placed,
             placed,
-            pltpu.VMEM(enc_weight.shape, BF16),
-            pltpu.VMEM(dec_weight.shape, BF16),
             dma((4,)),
-            dma((2,)),
+            dma((4, halves)),
             dma((n,)),
             dma((n,)),
             dma((3, halves, n)),
@@ -471,8 +464,17 @@
         ),
     )(
         counts, active, tokens, target, enc_weight, dec_weight,
-        enc_bias.reshape(own // BLK, BLK), dec_bias.reshape(1, features),
+        enc_bias.reshape(own // BLK, BLK), dec_bias.reshape(features // BLK, BLK),
     )
+    depth = halves * n * high
+
+    def transposed_dot(left, right):
+        return lax.dot_general(
+            left.reshape(depth, left.shape[-1]), right.reshape(depth, right.shape[-1]),
+            (((0,), (0,)), ((), ())), preferred_element_type=F32,
+        ).astype(BF16)
+
+    return transposed_dot(rows_in, grads), transposed_dot(acts, errors_in)
 
 
 def solution(mesh):

time: 76.5 us -> 75.9 us (level)
  matrix products: 0 us -> 5.91 us
  local copies, waits for them, and re-layouts: 5.2 us -> 0.01 us
  Pallas kernels: 69.5 us -> 68.2 us
    dot_general x0 -> x2, matrix products: none -> 5.91 us  [transposed_dot(): lax.dot_general(left.reshape(depth, left.shape[-1]), right.reshape(depth,...]
    unnamed x4, local copies, waits for them, and re-layouts: 3.93 us -> 0.01 us
    pallas_call x1, Pallas kernels: 69.5 us -> 68.2 us  [local(): pl.pallas_call(functools.partial(kernel, n, n_dp, halves), out_shape=(arr...]
    reshape x1 -> x0, local copies, waits for them, and re-layouts: 1.27 us -> none  [local(): dec_bias.reshape(1, features)]
where the time goes in v3:
time: 75.9 us; the launch traced here: 74.7 us
  Pallas kernels  68.2 us (90%)
  matrix products  5.91 us (8%)
    pallas_call x1, Pallas kernels, local(): pl.pallas_call(functools.partial(kernel, n, n_dp, halves), out_shape=(arr...  68.2 us
    dot_general x2, matrix products, transposed_dot(): lax.dot_general(left.reshape(depth, left.shape[-1]), right.reshape(depth,...  5.91 us

profile of v3, /device:TPU:0, one launch (start us, length us, event | category | flops | bytes accessed | tf_op | source)
XLA Modules:
  0.0 74.7 jit_solution(7025701489814796734)
XLA Ops:
  0.6 68.2 %shard_map.95 = (bf16[2,4,64,768]{3,2,1,0:T(8,128)(2,1)}, bf16[2,4,64,768]{3,2,1,0:T(8,128)(2,1)}, bf16[2,4,64,1024]{3,2,1,0:T(8,128)(2,1)}, bf16[2,4,64,1024]{3,2,1,0:T(8,128)(2,1)}) custom-call(s32[8]{0:T(128)} %counts.1, s32[8,8]{1,0:T(8,128)} %active.1, bf16[1024,768]{1,0:T(8,128)(2,1)} %tokens_any.1, bf16[1024,768]{1,0:T(8,128)(2,1)} %target_any.1, ...), custom_call_target="tpu_custom_call" | custom-call | tf_op jit(solution)/shard_map/pallas_call | solution.py:425
  68.8 0.0 copy-start
  68.8 0.0 copy-start.1
  68.8 3.7 %bitcast_convert_fusion.1 = bf16[768,1024]{1,0:T(8,128)(2,1)} fusion(bf16[2,4,64,768]{3,2,1,0:T(8,128)(2,1)} %get-tuple-element.6, bf16[2,4,64,1024]{3,2,1,0:T(8,128)(2,1)} %get-tuple-element.7), kind=kOutput, calls=%fused_computation.1 | convolution fusion | flops 806092800 | bytes 3407872 | tf_op jit(solution)/shard_map/dot_general | solution.py:472
  72.6 0.0 copy-done
  72.6 0.0 copy-done.1
  72.6 2.2 %bitcast_convert_fusion = bf16[1024,768]{1,0:T(8,128)(2,1)} fusion(bf16[2,4,64,1024]{3,2,1,0:T(8,128)(2,1)S(1)} %copy-done, bf16[2,4,64,768]{3,2,1,0:T(8,128)(2,1)S(1)} %copy-done.1), kind=kOutput, calls=%fused_computation | convolution fusion | flops 806092800 | bytes 3407872 | tf_op jit(solution)/shard_map/dot_general | solution.py:472
Async XLA Ops:
  68.8 3.8 %copy-start = (bf16[2,4,64,1024]{3,2,1,0:T(8,128)(2,1)S(1)}, bf16[2,4,64,1024]{3,2,1,0:T(8,128)(2,1)}, u32[]{:S(2)}) copy-start(bf16[2,4,64,1024]{3,2,1,0:T(8,128)(2,1)} %get-tuple-element.8) | copy-start | bytes 3145732
  68.8 3.8 %copy-start.1 = (bf16[2,4,64,768]{3,2,1,0:T(8,128)(2,1)S(1)}, bf16[2,4,64,768]{3,2,1,0:T(8,128)(2,1)}, u32[]{:S(2)}) copy-start(bf16[2,4,64,768]{3,2,1,0:T(8,128)(2,1)} %get-tuple-element.9) | copy-start | bytes 2359300

commit v4 on v3

--- a/solution.py
+++ b/solution.py
@@ -204,6 +204,8 @@
         if h == 0:
             pl.semaphore_wait(barrier, n - 1 + n_dp - 1)
             each(n - 1, lambda k: c_copy(k + 1).start())
+        if h > 0:
+            each(n - 1, lambda k, h=h: z_copy(TOK, h - 1, tok_send, tok, k + 1).wait_send())
         each(n - 1, lambda k, h=h: z_copy(TOK, h, tok_send, tok, k + 1).start())
     for h in range(halves):
         for at in range(0, high, 32):
@@ -386,7 +388,8 @@
             for phase, src, dst in (
                 (TOK, tok_send, tok), (PART, part_send, part), (ERR, err_send, err)
             ):
-                z_copy(phase, h, src, dst, k + 1).wait_send()
+                if phase != TOK or h == halves - 1:
+                    z_copy(phase, h, src, dst, k + 1).wait_send()
 
         def settle_d(k, h=h):
             for phase, src, dst in ((RS_PRE, pre_part, pre_in), (RS_BACK, back_part, back_in)):

time: 75.9 us -> 78.2 us (1.030); the launches traced: 74.7 us -> 78.1 us
  Pallas kernels: 68.2 us -> 71.5 us
    pallas_call x1, Pallas kernels: 68.2 us -> 71.5 us  [local(): pl.pallas_call(functools.partial(kernel, n, n_dp, halves), out_shape=(arr...]
where the time goes in v4:
time: 78.2 us; the launch traced here: 78.1 us
  Pallas kernels  71.5 us (91%)
  matrix products  5.91 us (8%)
    pallas_call x1, Pallas kernels, local(): pl.pallas_call(functools.partial(kernel, n, n_dp, halves), out_shape=(arr...  71.5 us
    dot_general x2, matrix products, transposed_dot(): lax.dot_general(left.reshape(depth, left.shape[-1]), right.reshape(depth,...  5.91 us

profile of v4, /device:TPU:0, one launch (start us, length us, event | category | flops | bytes accessed | tf_op | source)
XLA Modules:
  0.0 78.1 jit_solution(11348468723915752370)
XLA Ops:
  0.6 71.5 %shard_map.95 = (bf16[2,4,64,768]{3,2,1,0:T(8,128)(2,1)}, bf16[2,4,64,768]{3,2,1,0:T(8,128)(2,1)}, bf16[2,4,64,1024]{3,2,1,0:T(8,128)(2,1)}, bf16[2,4,64,1024]{3,2,1,0:T(8,128)(2,1)}) custom-call(s32[8]{0:T(128)} %counts.1, s32[8,8]{1,0:T(8,128)} %active.1, bf16[1024,768]{1,0:T(8,128)(2,1)} %tokens_any.1, bf16[1024,768]{1,0:T(8,128)(2,1)} %target_any.1, ...), custom_call_target="tpu_custom_call" | custom-call | tf_op jit(solution)/shard_map/pallas_call | solution.py:428
  72.1 0.0 copy-start
  72.1 0.0 copy-start.1
  72.1 3.7 %bitcast_convert_fusion.1 = bf16[768,1024]{1,0:T(8,128)(2,1)} fusion(bf16[2,4,64,768]{3,2,1,0:T(8,128)(2,1)} %get-tuple-element.6, bf16[2,4,64,1024]{3,2,1,0:T(8,128)(2,1)} %get-tuple-element.7), kind=kOutput, calls=%fused_computation.1 | convolution fusion | flops 806092800 | bytes 3407872 | tf_op jit(solution)/shard_map/dot_general | solution.py:475
  75.9 0.0 copy-done
  75.9 0.0 copy-done.1
  75.9 2.2 %bitcast_convert_fusion = bf16[1024,768]{1,0:T(8,128)(2,1)} fusion(bf16[2,4,64,1024]{3,2,1,0:T(8,128)(2,1)S(1)} %copy-done, bf16[2,4,64,768]{3,2,1,0:T(8,128)(2,1)S(1)} %copy-done.1), kind=kOutput, calls=%fused_computation | convolution fusion | flops 806092800 | bytes 3407872 | tf_op jit(solution)/shard_map/dot_general | solution.py:475
Async XLA Ops:
  72.1 3.8 %copy-start = (bf16[2,4,64,1024]{3,2,1,0:T(8,128)(2,1)S(1)}, bf16[2,4,64,1024]{3,2,1,0:T(8,128)(2,1)}, u32[]{:S(2)}) copy-start(bf16[2,4,64,1024]{3,2,1,0:T(8,128)(2,1)} %get-tuple-element.8) | copy-start | bytes 3145732
  72.1 3.8 %copy-start.1 = (bf16[2,4,64,768]{3,2,1,0:T(8,128)(2,1)S(1)}, bf16[2,4,64,768]{3,2,1,0:T(8,128)(2,1)}, u32[]{:S(2)}) copy-start(bf16[2,4,64,768]{3,2,1,0:T(8,128)(2,1)} %get-tuple-element.9) | copy-start | bytes 2359300
